TPU v7x, 32 devices: a whole 2x2x4 slice. The times are simulated.
32 devices in a mesh: groups: 2 (over x), seqa: 16 (over z, y, core).
Axes of the slice: x: 2, y: 2, z: 4, core: 2. Of those that a mesh axis runs over, the one named last changes fastest.
Arguments:
- inputs: bfloat16 [4096, 2048], P(('groups', 'seqa')), parts along dimension 0, may hold values from -6 to 6
- gate_in: bfloat16 [4096, 2048], P(('groups', 'seqa')), parts along dimension 0, may hold values from -6 to 6
- grad_out: bfloat16 [4096, 2048], P(('groups', 'seqa')), parts along dimension 0, may hold values from -6 to 6
- right_factor: bfloat16 [128, 128], replicated, may hold values from -0.5 to 0.5
- left_factor: bfloat16 [128, 16, 16], P('seqa'), may hold values from -1.5 to 1.5
Outputs:
- grad_inputs: bfloat16 [4096, 2048], P(('groups', 'seqa')), parts along dimension 0
- grad_gate: bfloat16 [4096, 2048], P(('groups', 'seqa')), parts along dimension 0
- grad_right: float32 [256, 128], P(('groups', 'seqa')), parts along dimension 0
- grad_left: float32 [256, 16, 16], P(('groups', 'seqa')), parts along dimension 0
There are 2 independent parts, one for each index of `groups`. A program takes and returns all parts, laid end to end along the dimension named above; an argument that names none is the same for every part. Nothing has to cross between parts.
All inputs are finite; a program needn't handle non-finite values.
Results may differ from a plain program's by a relative error of at most 0.0058.
Values may be sent and summed in bfloat16 or wider, within the bound.
A program may use at most 64 MiB of HBM per device.

v0:
```python
import jax
import jax.numpy as jnp
from jax import lax
from jax.sharding import PartitionSpec as P


def gate_grads(mixed, gate_in, grad_out):
    gate_f = gate_in.astype(jnp.float32)
    grad_f = grad_out.astype(jnp.float32)
    sig = jax.nn.sigmoid(gate_f)
    grad_mixed = (grad_f * gate_f * sig).astype(jnp.bfloat16)
    grad_gate = (grad_f * mixed.astype(jnp.float32) * sig * (1.0 + gate_f * (1.0 - sig))).astype(
        jnp.bfloat16
    )
    return (grad_mixed, grad_gate)


def shards(inputs, gate_in, grad_out, right_factor, left_factor):
    places = jnp.arange(right_factor.shape[0])
    mask_right = (places[:, None] >= places[None, :]).astype(right_factor.dtype)
    right_masked = right_factor * mask_right
    blocks = jnp.arange(left_factor.shape[1])
    mask_left = (blocks[:, None] >= blocks[None, :]).astype(left_factor.dtype)
    left_masked = left_factor * mask_left[None]
    first = jnp.dot(right_masked, inputs, preferred_element_type=jnp.float32).astype(jnp.bfloat16)
    first_cols = lax.all_to_all(first[None], "seqa", split_axis=1, concat_axis=0, tiled=True)
    second = jnp.einsum(
        "jpa,ajd->pjd", left_masked, first_cols, preferred_element_type=jnp.float32
    ).astype(jnp.bfloat16)
    mixed = lax.all_to_all(second, "seqa", split_axis=0, concat_axis=1, tiled=True)[0]
    grad_mixed, grad_gate = gate_grads(mixed, gate_in, grad_out)
    grad_cols = lax.all_to_all(grad_mixed[None], "seqa", split_axis=1, concat_axis=0, tiled=True)
    grad_first_cols = jnp.einsum(
        "jpa,pjd->ajd", left_masked, grad_cols, preferred_element_type=jnp.float32
    ).astype(jnp.bfloat16)
    grad_left = jnp.einsum(
        "pjd,ajd->jpa", grad_cols, first_cols, preferred_element_type=jnp.float32
    ) * mask_left[None].astype(jnp.float32)
    grad_first = lax.all_to_all(grad_first_cols, "seqa", split_axis=0, concat_axis=1, tiled=True)[0]
    grad_inputs = jnp.dot(right_masked.T, grad_first, preferred_element_type=jnp.float32).astype(
        jnp.bfloat16
    )
    mask_float = mask_right.astype(jnp.float32)
    term = lax.dot_general(
        grad_first, inputs, (((1,), (1,)), ((), ())), preferred_element_type=jnp.float32
    )
    grad_right = lax.psum_scatter(term * mask_float, "seqa", scatter_dimension=0, tiled=True)
    return (grad_inputs, grad_gate, grad_right, grad_left)


def solution(mesh):
    in_specs = (
        P(("groups", "seqa"), None),
        P(("groups", "seqa"), None),
        P(("groups", "seqa"), None),
        P(),
        P("seqa", None, None),
    )
    out_specs = (
        P(("groups", "seqa"), None),
        P(("groups", "seqa"), None),
        P(("groups", "seqa"), None),
        P(("groups", "seqa"), None, None),
    )
    return jax.shard_map(shards, mesh=mesh, in_specs=in_specs, out_specs=out_specs, check_vma=False)
```

profile of v0, /device:TPU:0, one launch (start us, length us, event | category | flops | bytes accessed | tf_op | source)
XLA Modules:
  0.0 197.6 jit_solution(7471261467602071986)
XLA Ops:
  7.2 0.0 copy-start
  7.2 1.0 copy-done
  8.2 1.0 fusion.1
  9.3 0.8 copy.52
  10.1 0.5 broadcast.30
  10.6 3.7 %reduce = bf16[128,2048]{1,0:T(8,128)(2,1)S(1)} reduce(bf16[128,1,2048]{2,1,0:T(2,128)(2,1)S(1)} %bitcast.35, bf16[]{:T(256)} %broadcast.30), dimensions={1}, to_apply=%bitcast.31.reduce_sub_computation | reduce | bytes 1048578
  14.3 1.3 reshape.52
  15.6 7.4 %all-to-all-start.2 = ((bf16[16,2,8192]{2,1,0:T(2,128)(2,1)}), bf16[16,2,8192]{2,1,0:T(2,128)(2,1)S(1)}, u32[]{:S(2)}, u32[]{:S(2)}) async-start(bf16[16,2,8192]{2,1,0:T(2,128)(2,1)} %reshape.52), calls=%async_computation.2 | async-start | bytes 1048576 | tf_op jit(solution)/shard_map/all_to_all | solution.py:26
  23.0 14.5 %all-to-all-done.2 = bf16[16,2,8192]{2,1,0:T(2,128)(2,1)S(1)} async-done(((bf16[16,2,8192]{2,1,0:T(2,128)(2,1)}), bf16[16,2,8192]{2,1,0:T(2,128)(2,1)S(1)}, u32[]{:S(2)}, u32[]{:S(2)}) %all-to-all-start.2) | async-done | bytes 524320 | tf_op jit(solution)/shard_map/all_to_all | solution.py:26
  37.5 0.5 reshape.53
  38.0 0.0 copy-start.3
  38.0 0.3 copy.50
  38.4 0.4 copy-done.3
  38.8 0.7 fusion.2
  39.5 0.3 copy.32
  39.8 0.0 copy-start.1
  39.8 0.0 copy-start.2
  39.8 18.5 %all_to_all.42 = bf16[16,8,2048]{2,1,0:T(8,128)(2,1)S(1)} all-to-all(bf16[16,8,2048]{2,1,0:T(8,128)(2,1)S(1)} %copy.32), channel_id=1, replica_groups=mesh['groups'=2,'seqa'=16] {'seqa'}, dimensions={0} | all-to-all | bytes 1048576 | tf_op jit(solution)/shard_map/all_to_all | solution.py:30
  58.3 0.0 copy-done.1
  58.3 0.0 copy-done.2
  58.3 1.3 fusion.5
  59.6 0.8 copy.53
  60.5 4.0 %reduce.1 = bf16[128,2048]{1,0:T(8,128)(2,1)S(1)} reduce(bf16[128,1,2048]{2,1,0:T(2,128)(2,1)S(1)} %bitcast.36, bf16[]{:T(256)} %broadcast.30), dimensions={1}, to_apply=%bitcast.32.reduce_sub_computation | reduce | bytes 1048578
  64.4 0.5 reshape.50
  65.0 18.4 %all_to_all.43 = bf16[16,2,8192]{2,1,0:T(2,128)(2,1)S(1)} all-to-all(bf16[16,2,8192]{2,1,0:T(2,128)(2,1)S(1)} %reshape.50), channel_id=1, replica_groups=mesh['groups'=2,'seqa'=16] {'seqa'}, dimensions={0} | all-to-all | bytes 1048576 | tf_op jit(solution)/shard_map/all_to_all | solution.py:32
  83.3 0.5 reshape.51
  83.9 0.3 copy.51
  84.2 0.7 fusion
  84.9 1.1 copy.29
  86.0 4.1 %all-to-all-start.1 = ((bf16[16,8,2048]{2,1,0:T(8,128)(2,1)}), bf16[16,8,2048]{2,1,0:T(8,128)(2,1)S(1)}, u32[]{:S(2)}, u32[]{:S(2)}) async-start(bf16[16,8,2048]{2,1,0:T(8,128)(2,1)} %copy.29), calls=%async_computation.1 | async-start | bytes 1048576 | tf_op jit(solution)/shard_map/all_to_all | solution.py:39
  90.1 0.0 all-reduce.3.cloned.1.call-start
  90.1 0.0 copy-start.5
  90.1 0.6 copy-done.5
  90.8 0.6 dynamic-slice
  92.0 1.3 convolution_multiply_fusion
  93.3 11.2 %all-to-all-done.1 = bf16[16,8,2048]{2,1,0:T(8,128)(2,1)S(1)} async-done(((bf16[16,8,2048]{2,1,0:T(8,128)(2,1)}), bf16[16,8,2048]{2,1,0:T(8,128)(2,1)S(1)}, u32[]{:S(2)}, u32[]{:S(2)}) %all-to-all-start.1) | async-done | bytes 524320 | tf_op jit(solution)/shard_map/all_to_all | solution.py:39
  104.5 0.9 convolution_multiply_fusion.1
  105.4 0.0 copy-start.4
  105.5 0.0 all-reduce.3.cloned.1.call-update
  105.5 0.7 copy-done.4
  106.2 1.1 convolution_convert_fusion.2
  107.3 82.2 %all-reduce.3.cloned.1.call-done = f32[128,128]{1,0:T(8,128)} async-done(((f32[128,128]{1,0:T(8,128)}), f32[128,128]{1,0:T(8,128)}) %all-reduce.3.cloned.1.call-update) | async-done | bytes 65552
  189.5 1.3 constant_dynamic-slice_fusion
  (2 shorter events, 0.0 us)
Async XLA Ops:
  7.2 1.0 copy-start
  15.6 21.9 %all-to-all-start.2 = ((bf16[16,2,8192]{2,1,0:T(2,128)(2,1)}), bf16[16,2,8192]{2,1,0:T(2,128)(2,1)S(1)}, u32[]{:S(2)}, u32[]{:S(2)}) async-start(bf16[16,2,8192]{2,1,0:T(2,128)(2,1)} %reshape.52), calls=%async_computation.2 | async-start | bytes 1048576 | tf_op jit(solution)/shard_map/all_to_all | solution.py:26
  38.0 0.8 copy-start.3
  39.8 18.5 %copy-start.1 = (bf16[128,2048]{1,0:T(8,128)(2,1)S(1)}, bf16[128,2048]{1,0:T(8,128)(2,1)}, u32[]{:S(2)}) copy-start(bf16[128,2048]{1,0:T(8,128)(2,1)} %param.7) | copy-start | bytes 1572868
  39.8 18.5 %copy-start.2 = (bf16[128,2048]{1,0:T(8,128)(2,1)S(1)}, bf16[128,2048]{1,0:T(8,128)(2,1)}, u32[]{:S(2)}) copy-start(bf16[128,2048]{1,0:T(8,128)(2,1)} %param.6) | copy-start | bytes 1572868
  86.0 18.6 %all-to-all-start.1 = ((bf16[16,8,2048]{2,1,0:T(8,128)(2,1)}), bf16[16,8,2048]{2,1,0:T(8,128)(2,1)S(1)}, u32[]{:S(2)}, u32[]{:S(2)}) async-start(bf16[16,8,2048]{2,1,0:T(8,128)(2,1)} %copy.29), calls=%async_computation.1 | async-start | bytes 1048576 | tf_op jit(solution)/shard_map/all_to_all | solution.py:39
  90.1 99.4 %all-reduce.3.cloned.1.call-start = ((), (), s32[]{:S(2)}) async-start(), calls=%async_computation.4 | async-start | bytes 131072
  90.1 0.7 copy-start.5
  105.4 0.8 copy-start.4
Sparse Core Ops, SparseCore 0:
  105.6 83.8 all-reduce.2
where the time goes:
time: 199 us; the launch traced here: 198 us
  waiting for transfers between devices  108 us (54%)
  blocking collectives  36.9 us (19%)
  between operations  14.8 us (7%)
  local copies, waits for them, and re-layouts  11.8 us (6%)
  starting transfers between devices  11.5 us (6%)
  other arithmetic  9.03 us (5%)
  matrix products  5.72 us (3%)
    unnamed x2, waiting for transfers between devices  82.2 us
    all_to_all x1, blocking collectives, shards(): lax.all_to_all(second, 'seqa', split_axis=0, concat_axis=1, tiled=True)[0]  18.5 us
    all_to_all x1, blocking collectives, shards(): lax.all_to_all(grad_mixed[None], 'seqa', split_axis=1, concat_axis=0, til...  18.4 us
    all_to_all x1, waiting for transfers between devices, shards(): lax.all_to_all(first[None], 'seqa', split_axis=1, concat_axis=0, tiled=True)  14.5 us
    all_to_all x1, waiting for transfers between devices, shards(): lax.all_to_all(grad_first_cols, 'seqa', split_axis=0, concat_axis=1, tile...  11.2 us
    unnamed x21, local copies, waits for them, and re-layouts  8.78 us
    unnamed x2, other arithmetic  7.67 us
    all_to_all x1, starting transfers between devices, shards(): lax.all_to_all(first[None], 'seqa', split_axis=1, concat_axis=0, tiled=True)  7.39 us
  transfers between devices with their start and end apart: 3, of which 3 were waited for; matrix products, arithmetic and copies ran while one was open for 2% of the time, Pallas kernels for 0%

commit v1 on v0

--- a/solution.py
+++ b/solution.py
@@ -1,7 +1,13 @@
+import functools
+
 import jax
 import jax.numpy as jnp
 from jax import lax
+from jax.experimental import pallas as pl
+from jax.experimental.pallas import tpu as pltpu
 from jax.sharding import PartitionSpec as P
+
+F32, BF16 = jnp.float32, jnp.bfloat16
 
 
 def gate_grads(mixed, gate_in, grad_out):
@@ -15,7 +21,7 @@
     return (grad_mixed, grad_gate)
 
 
-def shards(inputs, gate_in, grad_out, right_factor, left_factor):
+def plain_shards(inputs, gate_in, grad_out, right_factor, left_factor):
     places = jnp.arange(right_factor.shape[0])
     mask_right = (places[:, None] >= places[None, :]).astype(right_factor.dtype)
     right_masked = right_factor * mask_right
@@ -48,7 +54,215 @@
     return (grad_inputs, grad_gate, grad_right, grad_left)
 
 
+def iota(shape, dim):
+    return lax.broadcasted_iota(jnp.int32, shape, dim)
+
+
+def dot(a, b, dims=((1,), (0,)), **kw):
+    return lax.dot_general(a, b, (dims, ((), ())), preferred_element_type=F32, **kw)
+
+
+def kernel(
+    n, parts, x_ref, gate_ref, gout_ref, right_ref, left_ref,
+    gx_ref, ggate_ref, gright_ref, gleft_ref,
+    out_buf, in_buf, term_buf, sum_buf, weights, send_sem, recv_sem, tsend_sem, trecv_sem,
+):
+    me = lax.axis_index("seqa")
+    rows, width = x_ref.shape
+    r = rows // n
+    half = width // 2
+    w = half // parts
+    barrier = pltpu.get_barrier_semaphore()
+
+    def partner(k):
+        return lax.rem(me + k, n)
+
+    @pl.loop(1, n)
+    def _(k):
+        pl.semaphore_signal(
+            barrier, inc=1, device_id={"seqa": partner(k)}, device_id_type=pl.DeviceIdType.MESH
+        )
+
+    def copy(kind, part, to):
+        return pltpu.make_async_remote_copy(
+            src_ref=out_buf.at[kind, part, to],
+            dst_ref=in_buf.at[kind, part, me],
+            send_sem=send_sem.at[kind, part, to],
+            recv_sem=recv_sem.at[kind, part, me],
+            device_id={"seqa": to},
+            device_id_type=pl.DeviceIdType.MESH,
+        )
+
+    def arrival(kind, part, src):
+        return pltpu.make_async_remote_copy(
+            src_ref=out_buf.at[kind, part, src],
+            dst_ref=in_buf.at[kind, part, src],
+            send_sem=send_sem.at[kind, part, src],
+            recv_sem=recv_sem.at[kind, part, src],
+            device_id={"seqa": src},
+            device_id_type=pl.DeviceIdType.MESH,
+        )
+
+    def send_all(kinds, part):
+        @pl.loop(1, n)
+        def _(k):
+            for kind in kinds:
+                copy(kind, part, partner(k)).start()
+
+    def wait_all(kinds, part):
+        @pl.loop(1, n)
+        def _(k):
+            src = lax.rem(me + n - k, n)
+            for kind in kinds:
+                arrival(kind, part, src).wait_recv()
+
+    def columns(part, h):
+        return pl.ds(h * half + part * w, w)
+
+    def pack(v0, v1):
+        both = jnp.concatenate([v0.reshape(n, r, w), v1.reshape(n, r, w)], axis=1)
+        return both.astype(BF16)
+
+    def unpack(v):
+        v = v.astype(F32)
+        return v[:, :r].reshape(rows, w), v[:, r:].reshape(rows, w)
+
+    causal = iota((rows, rows), 0) >= iota((rows, rows), 1)
+    rm = jnp.where(causal, right_ref[...].astype(F32), 0.0).astype(BF16)
+
+    for part in range(parts):
+        vals = [dot(rm, x_ref[:, columns(part, h)]) for h in range(2)]
+        out_buf[0, part] = pack(*vals)
+        vals = []
+        for h in range(2):
+            gate = gate_ref[:, columns(part, h)].astype(F32)
+            gout = gout_ref[:, columns(part, h)].astype(F32)
+            vals.append(gout * gate * jax.nn.sigmoid(gate))
+        out_buf[1, part] = pack(*vals)
+        if part == 0:
+            pl.semaphore_wait(barrier, n - 1)
+        send_all((0, 1), part)
+
+    c = n * 2 * r
+    row, col = iota((c, n * r), 0), iota((c, n * r), 1)
+    pick = (col == (row % r) * n + row // (2 * r)).astype(BF16)
+    spread = (iota((n, c), 1) // (2 * r) == iota((n, c), 0)).astype(BF16)
+    row, col = iota((c, c), 0), iota((c, c), 1)
+    keep = (row % (2 * r) == col % (2 * r)) & (row // (2 * r) >= col // (2 * r))
+    wide = dot(dot(pick, left_ref[...]).astype(BF16), spread)
+    weights[...] = jnp.where(keep, wide, 0.0).astype(BF16)
+
+    gram = jnp.zeros((c, c), F32)
+    for part in range(parts):
+        wait_all((0, 1), part)
+        for kind in range(2):
+            in_buf[kind, part, me] = out_buf[kind, part, me]
+        f = in_buf[0, part].reshape(c, w)
+        g = in_buf[1, part].reshape(c, w)
+        out_buf[2, part] = dot(weights[...], f).astype(BF16).reshape(n, 2 * r, w)
+        out_buf[3, part] = dot(weights[...], g, ((0,), (0,))).astype(BF16).reshape(n, 2 * r, w)
+        send_all((3, 2), part)
+        gram = gram + dot(g, f, ((1,), (1,)))
+    gram = jnp.where(keep, gram, 0.0)
+    best = lax.Precision.HIGHEST
+    narrow = dot(gram, spread.astype(F32), ((1,), (1,)), precision=best)
+    gleft_ref[...] = dot(pick.astype(F32), narrow, ((0,), (0,)), precision=best)
+
+    term = jnp.zeros((rows, rows), F32)
+    for part in range(parts):
+        wait_all((2, 3), part)
+        for kind in range(2, 4):
+            in_buf[kind, part, me] = out_buf[kind, part, me]
+        vals = [v.astype(BF16) for v in unpack(in_buf[3, part])]
+        for h in range(2):
+            term = term + dot(vals[h], x_ref[:, columns(part, h)], ((1,), (1,)))
+        if part == parts - 1:
+            term_buf[...] = jnp.where(causal, term, 0.0).reshape(n, r, rows)
+
+            def term_copy(to, slot):
+                return pltpu.make_async_remote_copy(
+                    src_ref=term_buf.at[to],
+                    dst_ref=sum_buf.at[slot],
+                    send_sem=tsend_sem.at[to],
+                    recv_sem=trecv_sem.at[slot],
+                    device_id={"seqa": to},
+                    device_id_type=pl.DeviceIdType.MESH,
+                )
+
+            @pl.loop(1, n)
+            def _(k):
+                term_copy(partner(k), me).start()
+
+        for h in range(2):
+            gx_ref[:, columns(part, h)] = dot(rm, vals[h], ((0,), (0,))).astype(BF16)
+        for h, mixed in enumerate(unpack(in_buf[2, part])):
+            gate = gate_ref[:, columns(part, h)].astype(F32)
+            gout = gout_ref[:, columns(part, h)].astype(F32)
+            sig = jax.nn.sigmoid(gate)
+            ggate_ref[:, columns(part, h)] = (
+                gout * mixed * sig * (1.0 + gate * (1.0 - sig))
+            ).astype(BF16)
+
+    @pl.loop(1, n)
+    def _(k):
+        src = lax.rem(me + n - k, n)
+        term_copy(src, src).wait_recv()
+
+    sum_buf[me] = term_buf[me]
+    gright_ref[...] = jnp.sum(sum_buf[...], axis=0)
+
+    @pl.loop(1, n)
+    def _(k):
+        to = partner(k)
+        for part in range(parts):
+            for kind in range(4):
+                copy(kind, part, to).wait_send()
+        term_copy(to, me).wait_send()
+
+
+def fused_shards(n, parts, inputs, gate_in, grad_out, right_factor, left_factor):
+    rows, width = inputs.shape
+    r = rows // n
+    w = width // 2 // parts
+    left2 = left_factor.reshape(r * n, n)
+    vmem = pl.BlockSpec(memory_space=pltpu.VMEM)
+    gx, gg, gr, gl = pl.pallas_call(
+        functools.partial(kernel, n, parts),
+        out_shape=(
+            jax.ShapeDtypeStruct(inputs.shape, BF16),
+            jax.ShapeDtypeStruct(inputs.shape, BF16),
+            jax.ShapeDtypeStruct((r, rows), F32),
+            jax.ShapeDtypeStruct((r * n, n), F32),
+        ),
+        in_specs=[vmem] * 5,
+        out_specs=(vmem,) * 4,
+        scratch_shapes=[
+            pltpu.VMEM((4, parts, n, 2 * r, w), BF16),
+            pltpu.VMEM((4, parts, n, 2 * r, w), BF16),
+            pltpu.VMEM((n, r, rows), F32),
+            pltpu.VMEM((n, r, rows), F32),
+            pltpu.VMEM((2 * r * n, 2 * r * n), BF16),
+            pltpu.SemaphoreType.DMA((4, parts, n)),
+            pltpu.SemaphoreType.DMA((4, parts, n)),
+            pltpu.SemaphoreType.DMA((n,)),
+            pltpu.SemaphoreType.DMA((n,)),
+        ],
+        compiler_params=pltpu.CompilerParams(
+            collective_id=0, has_side_effects=True, vmem_limit_bytes=40 * 2**20
+        ),
+    )(inputs, gate_in, grad_out, right_factor, left2)
+    return gx, gg, gr, gl.reshape(r, n, n)
+
+
 def solution(mesh):
+    n = mesh.shape["seqa"]
+
+    def shards(inputs, gate_in, grad_out, right_factor, left_factor):
+        rows = inputs.shape[0]
+        if rows == 8 * n and left_factor.shape == (8, n, n):
+            return fused_shards(n, 2, inputs, gate_in, grad_out, right_factor, left_factor)
+        return plain_shards(inputs, gate_in, grad_out, right_factor, left_factor)
+
     in_specs = (
         P(("groups", "seqa"), None),
         P(("groups", "seqa"), None),

time: 199 us -> 69.6 us (0.35)
  waiting for transfers between devices: 108 us -> 0 us
  Pallas kernels: 0 us -> 61.1 us
  blocking collectives: 36.9 us -> 0 us
  between operations: 14.8 us -> 0.65 us
  starting transfers between devices: 11.5 us -> 0 us
  other arithmetic: 9.03 us -> 0 us
  matrix products: 5.72 us -> 0 us
  local copies, waits for them, and re-layouts: 11.8 us -> 7.44 us
    unnamed x2 -> x0, waiting for transfers between devices: 82.2 us -> none
    pallas_call x0 -> x1, Pallas kernels: none -> 61.1 us  [fused_shards(): pl.pallas_call(functools.partial(kernel, n, parts), out_shape=(jax.ShapeD...]
    all_to_all x2 -> x0, blocking collectives: 36.9 us -> none  [the longest x1 18.5 us: shards(): lax.all_to_all(second, 'seqa', split_axis=0, concat_axis=1, tiled=True)[0]]
    all_to_all x2 -> x0, waiting for transfers between devices: 25.7 us -> none  [the longest x1 14.5 us: shards(): lax.all_to_all(first[None], 'seqa', split_axis=1, concat_axis=0, tiled=True)]
    all_to_all x2 -> x0, starting transfers between devices: 11.5 us -> none  [the longest x1 7.39 us: shards(): lax.all_to_all(first[None], 'seqa', split_axis=1, concat_axis=0, tiled=True)]
    unnamed x2 -> x0, other arithmetic: 7.67 us -> none
    dot_general x6 -> x0, matrix products: 5.72 us -> none  [the longest x1 1.29 us: shards(): jnp.einsum('pjd,ajd->jpa', grad_cols, first_cols, preferred_element_type=...]
    unnamed x21 -> x14, local copies, waits for them, and re-layouts: 8.78 us -> 7.44 us
  transfers between devices with their start and end apart: 3 -> 0, of which waited for: 3 -> 0; matrix products, arithmetic and copies ran while one was open for 2% -> 0% of each run, Pallas kernels for 0% -> 0%
where the time goes in v1:
time: 69.6 us; the launch traced here: 69.2 us
  Pallas kernels  61.1 us (88%)
  local copies, waits for them, and re-layouts  7.44 us (11%)
    pallas_call x1, Pallas kernels, fused_shards(): pl.pallas_call(functools.partial(kernel, n, parts), out_shape=(jax.ShapeD...  61.1 us
    unnamed x14, local copies, waits for them, and re-layouts  7.44 us

profile of v1, /device:TPU:0, one launch (start us, length us, event | category | flops | bytes accessed | tf_op | source)
XLA Modules:
  0.0 69.2 jit_solution(16562560715871535768)
XLA Ops:
  0.6 0.0 copy-start
  0.6 1.0 %copy-done = bf16[128,2048]{1,0:T(8,128)(2,1)S(1)} copy-done((bf16[128,2048]{1,0:T(8,128)(2,1)S(1)}, bf16[128,2048]{1,0:T(8,128)(2,1)}, u32[]{:S(2)}) %copy-start) | copy-done | bytes 524312
  1.7 0.0 copy-start.1
  1.7 1.0 %copy-done.1 = bf16[128,2048]{1,0:T(8,128)(2,1)S(1)} copy-done((bf16[128,2048]{1,0:T(8,128)(2,1)S(1)}, bf16[128,2048]{1,0:T(8,128)(2,1)}, u32[]{:S(2)}) %copy-start.1) | copy-done | bytes 524312
  2.7 0.0 copy-start.2
  2.7 1.0 %copy-done.2 = bf16[128,2048]{1,0:T(8,128)(2,1)S(1)} copy-done((bf16[128,2048]{1,0:T(8,128)(2,1)S(1)}, bf16[128,2048]{1,0:T(8,128)(2,1)}, u32[]{:S(2)}) %copy-start.2) | copy-done | bytes 524312
  3.8 0.0 copy-start.3
  3.8 0.8 %copy-done.3 = bf16[128,128]{1,0:T(8,128)(2,1)S(1)} copy-done((bf16[128,128]{1,0:T(8,128)(2,1)S(1)}, bf16[128,128]{1,0:T(8,128)(2,1)}, u32[]{:S(2)}) %copy-start.3) | copy-done | bytes 32792
  4.5 0.0 copy-start.4
  4.5 0.8 %copy-done.4 = bf16[8,16,16]{2,1,0:T(8,128)(2,1)S(1)} copy-done((bf16[8,16,16]{2,1,0:T(8,128)(2,1)S(1)}, bf16[8,16,16]{2,1,0:T(8,128)(2,1)}, u32[]{:S(2)}) %copy-start.4) | copy-done | bytes 4120
  5.3 61.1 %shard_map.84 = (bf16[128,2048]{1,0:T(8,128)(2,1)S(1)}, bf16[128,2048]{1,0:T(8,128)(2,1)S(1)}, f32[8,128]{1,0:T(8,128)S(1)}, f32[128,16]{1,0:T(8,128)S(1)}) custom-call(bf16[128,2048]{1,0:T(8,128)(2,1)S(1)} %copy-done, bf16[128,2048]{1,0:T(8,128)(2,1)S(1)} %copy-done.1, bf16[128,2048]{1,0:T(8,128)(2,1)S(1)} %copy-done.2, bf16[128,128]{1,0:T(8,128)(2,1)S(1)} %copy-done.3, ...), custom_call_target="tpu_custom_call" | custom-call | tf_op jit(solution)/shard_map/pallas_call | solution.py:229
  66.4 0.8 %copy.13 = bf16[128,2048]{1,0:T(8,128)(2,1)} copy(bf16[128,2048]{1,0:T(8,128)(2,1)S(1)} %get-tuple-element.16) | data formatting | bytes 1048576
  67.2 0.8 %copy.14 = bf16[128,2048]{1,0:T(8,128)(2,1)} copy(bf16[128,2048]{1,0:T(8,128)(2,1)S(1)} %get-tuple-element.17) | data formatting | bytes 1048576
  68.0 0.6 copy.15
  68.6 0.6 copy.16
Async XLA Ops:
  0.6 1.0 %copy-start = (bf16[128,2048]{1,0:T(8,128)(2,1)S(1)}, bf16[128,2048]{1,0:T(8,128)(2,1)}, u32[]{:S(2)}) copy-start(bf16[128,2048]{1,0:T(8,128)(2,1)} %x_ref.1) | copy-start | bytes 1572868
  1.7 1.0 %copy-start.1 = (bf16[128,2048]{1,0:T(8,128)(2,1)S(1)}, bf16[128,2048]{1,0:T(8,128)(2,1)}, u32[]{:S(2)}) copy-start(bf16[128,2048]{1,0:T(8,128)(2,1)} %gate_ref.1) | copy-start | bytes 1572868
  2.7 1.0 %copy-start.2 = (bf16[128,2048]{1,0:T(8,128)(2,1)S(1)}, bf16[128,2048]{1,0:T(8,128)(2,1)}, u32[]{:S(2)}) copy-start(bf16[128,2048]{1,0:T(8,128)(2,1)} %gout_ref.1) | copy-start | bytes 1572868
  3.8 0.8 %copy-start.3 = (bf16[128,128]{1,0:T(8,128)(2,1)S(1)}, bf16[128,128]{1,0:T(8,128)(2,1)}, u32[]{:S(2)}) copy-start(bf16[128,128]{1,0:T(8,128)(2,1)} %right_ref.1) | copy-start | bytes 98308
  4.5 0.8 %copy-start.4 = (bf16[8,16,16]{2,1,0:T(8,128)(2,1)S(1)}, bf16[8,16,16]{2,1,0:T(8,128)(2,1)}, u32[]{:S(2)}) copy-start(bf16[8,16,16]{2,1,0:T(8,128)(2,1)} %param.9) | copy-start | bytes 12292

commit v2 on v0

--- a/solution.py
+++ b/solution.py
@@ -1,7 +1,15 @@
+import functools
+
 import jax
 import jax.numpy as jnp
 from jax import lax
+from jax.experimental import pallas as pl
+from jax.experimental.pallas import tpu as pltpu
 from jax.sharding import PartitionSpec as P
+
+F32, BF16 = jnp.float32, jnp.bfloat16
+PARTS = 4
+SUMS = F32
 
 
 def gate_grads(mixed, gate_in, grad_out):
@@ -15,7 +23,7 @@
     return (grad_mixed, grad_gate)
 
 
-def shards(inputs, gate_in, grad_out, right_factor, left_factor):
+def plain_shards(inputs, gate_in, grad_out, right_factor, left_factor):
     places = jnp.arange(right_factor.shape[0])
     mask_right = (places[:, None] >= places[None, :]).astype(right_factor.dtype)
     right_masked = right_factor * mask_right
@@ -48,7 +56,436 @@
     return (grad_inputs, grad_gate, grad_right, grad_left)
 
 
+def iota(shape, dim):
+    return lax.broadcasted_iota(jnp.int32, shape, dim)
+
+
+def dot(a, b, dims=((1,), (0,)), **kw):
+    return lax.dot_general(a, b, (dims, ((), ())), preferred_element_type=F32, **kw)
+
+
+PLANES = 4
+PEERS = 4
+
+
+def kernel(
+    parts, x_hbm, gate_hbm, gout_hbm, right_hbm, left_hbm,
+    gx_ref, ggate_ref, gright_ref, gleft_ref,
+    x_ref, gate_ref, gout_ref, right_ref, left_ref,
+    cols_out, cols, back_out, back_in, sums_out, sums_in, weights, gram, term,
+    left_out, left_in, gl_out, gl_in, term_out, term_in,
+    load_sem, a_send, a_recv, relay_send, relay_recv, sum_send, sum_recv, b_send, b_recv,
+    left_send, left_recv, gl_send, gl_recv, t_send, t_recv,
+):
+    n = PLANES * PEERS
+    me = lax.axis_index("seqa")
+    z, i = me // PEERS, me % PEERS
+    rows, width = x_ref.shape
+    jj = rows // PEERS
+    w = width // parts
+    m = PEERS * jj
+    barrier = pltpu.get_barrier_semaphore()
+
+    def remote(src, dst, send, recv, to):
+        return pltpu.make_async_remote_copy(
+            src_ref=src, dst_ref=dst, send_sem=send, recv_sem=recv,
+            device_id={"seqa": to}, device_id_type=pl.DeviceIdType.MESH,
+        )
+
+    @pl.loop(1, n)
+    def _(k):
+        pl.semaphore_signal(
+            barrier, inc=1, device_id={"seqa": lax.rem(me + k, n)},
+            device_id_type=pl.DeviceIdType.MESH,
+        )
+
+    pairs = (
+        (x_hbm, x_ref), (right_hbm, right_ref), (gate_hbm, gate_ref),
+        (gout_hbm, gout_ref), (left_hbm, left_ref),
+    )
+    loads = [pltpu.make_async_copy(a, b, load_sem.at[k]) for k, (a, b) in enumerate(pairs)]
+    for load in loads:
+        load.start()
+
+    def columns(c):
+        return pl.ds(pl.multiple_of(c * w, w), w)
+
+    causal = iota((rows, rows), 0) >= iota((rows, rows), 1)
+
+    def rm():
+        return jnp.where(causal, right_ref[...].astype(F32), 0.0).astype(BF16)
+
+    def block(kind, c, q):
+        return cols.at[kind, c, pl.ds(PEERS * q, PEERS)]
+
+    def planes(kind, c, lo, hi):
+        return cols[kind, c, PEERS * lo : PEERS * hi].reshape((hi - lo) * m, w)
+
+    def w_block(p0, p1, q0, q1):
+        return weights[m * p0 : m * p1, m * q0 : m * q1]
+
+    def a_copy(kind, c, p):
+        return remote(
+            cols_out.at[kind, c, p], cols.at[kind, c, me],
+            a_send.at[kind, c, p], a_recv.at[kind, c, i], PEERS * z + p,
+        )
+
+    def a_arrival(kind, c, p):
+        return remote(
+            cols_out.at[kind, c, p], cols.at[kind, c, PEERS * z + p],
+            a_send.at[kind, c, p], a_recv.at[kind, c, p], PEERS * z + p,
+        )
+
+    def compute_a(c):
+        first = dot(rm(), x_ref[:, columns(c)])
+        cols_out[0, c] = first.astype(BF16).reshape(PEERS, jj, w)
+        gate = gate_ref[:, columns(c)].astype(F32)
+        gout = gout_ref[:, columns(c)].astype(F32)
+        mixed_grad = gout * gate * jax.nn.sigmoid(gate)
+        cols_out[1, c] = mixed_grad.astype(BF16).reshape(PEERS, jj, w)
+
+    def send_a(c):
+        for k in range(1, PEERS):
+            for kind in range(2):
+                a_copy(kind, c, lax.rem(i + k, PEERS)).start()
+        for kind in range(2):
+            cols[kind, c, me] = cols_out[kind, c, i]
+
+    relays = {0: (0, (1, 2)), 1: (0, (2,)), 2: (1, (1,)), 3: (1, (2, 1))}
+
+    def relay(kind, c, q, slot, to_plane):
+        return remote(
+            block(kind, c, q), block(kind, c, q),
+            relay_send.at[c, slot], relay_recv.at[kind, c, q], PEERS * to_plane + i,
+        )
+
+    def sums(c, to_plane):
+        return remote(
+            sums_out.at[c], sums_in.at[c], sum_send.at[c], sum_recv.at[c], PEERS * to_plane + i
+        )
+
+    def b_copy(kind, c, p, slot):
+        return remote(
+            back_out.at[kind, c, p], back_in.at[kind, c, slot],
+            b_send.at[kind, c, p], b_recv.at[kind, c, slot], PEERS * z + p,
+        )
+
+    def send_back(kind, c, value):
+        back_out[kind, c] = value.astype(BF16).reshape(PEERS, jj, w)
+        for k in range(1, PEERS):
+            b_copy(kind, c, lax.rem(i + k, PEERS), i).start()
+        back_in[kind, c, i] = back_out[kind, c, i]
+
+    def add_gram(c, p0, p1, q0, q1):
+        gram[m * p0 : m * p1, m * q0 : m * q1] += dot(
+            planes(1, c, p0, p1), planes(0, c, q0, q1), ((1,), (1,))
+        )
+
+    def stage_b(c):
+        for k in range(1, PEERS):
+            for kind in range(2):
+                a_arrival(kind, c, lax.rem(i + PEERS - k, PEERS)).wait_recv()
+        for q, (kind, targets) in relays.items():
+
+            @pl.when(z == q)
+            def _(q=q, kind=kind, targets=targets):
+                for slot, to_plane in enumerate(targets):
+                    relay(kind, c, q, slot, to_plane).start()
+                if q == 0:
+                    send_back(0, c, dot(w_block(0, 1, 0, 1), planes(0, c, 0, 1)))
+                    add_gram(c, 0, 1, 0, 1)
+                if q == 3:
+                    send_back(1, c, dot(w_block(3, 4, 3, 4), planes(1, c, 3, 4), ((0,), (0,))))
+                    add_gram(c, 3, 4, 3, 4)
+
+    def stage_d(c):
+        @pl.when(z == 1)
+        def _():
+            relay(0, c, 0, 0, 0).wait_recv()
+            send_back(0, c, dot(w_block(1, 2, 0, 2), planes(0, c, 0, 2)))
+            relay(1, c, 2, 0, 2).wait_recv()
+            relay(1, c, 3, 0, 3).wait_recv()
+            g = planes(1, c, 1, 4)
+            sums_out[c] = dot(w_block(1, 4, 0, 1), g, ((0,), (0,))).reshape(PEERS, jj, w)
+            sums(c, 0).start()
+            send_back(1, c, dot(w_block(1, 4, 1, 2), g, ((0,), (0,))))
+            add_gram(c, 1, 4, 0, 1)
+            add_gram(c, 1, 2, 1, 2)
+
+        @pl.when(z == 2)
+        def _():
+            relay(1, c, 3, 0, 3).wait_recv()
+            send_back(1, c, dot(w_block(2, 4, 2, 3), planes(1, c, 2, 4), ((0,), (0,))))
+            relay(0, c, 1, 0, 1).wait_recv()
+            relay(0, c, 0, 0, 0).wait_recv()
+            f = planes(0, c, 0, 3)
+            sums_out[c] = dot(w_block(3, 4, 0, 3), f).reshape(PEERS, jj, w)
+            sums(c, 3).start()
+            send_back(0, c, dot(w_block(2, 3, 0, 3), f))
+            add_gram(c, 2, 4, 1, 3)
+
+    def stage_s(c):
+        @pl.when(z == 0)
+        def _():
+            own = dot(w_block(0, 1, 0, 1), planes(1, c, 0, 1), ((0,), (0,)))
+            sums(c, 1).wait_recv()
+            send_back(1, c, own + sums_in[c].reshape(m, w))
+
+        @pl.when(z == 3)
+        def _():
+            own = dot(w_block(3, 4, 3, 4), planes(0, c, 3, 4))
+            sums(c, 2).wait_recv()
+            send_back(0, c, own + sums_in[c].reshape(m, w))
+
+    def term_copy(to, slot):
+        return remote(term_out.at[to], term_in.at[slot], t_send.at[to], t_recv.at[slot], to)
+
+    def stage_e(c):
+        for k in range(1, PEERS):
+            p = lax.rem(i + PEERS - k, PEERS)
+            for kind in range(2):
+                b_copy(kind, c, p, p).wait_recv()
+        grad_first = back_in[1, c].reshape(rows, w)
+        term[...] += dot(grad_first, x_ref[:, columns(c)], ((1,), (1,)))
+
+        @pl.when(c == parts - 1)
+        def _():
+            term_out[...] = jnp.where(causal, term[...], 0.0).reshape(n, rows // n, rows)
+
+            @pl.loop(1, n)
+            def _(k):
+                term_copy(lax.rem(me + k, n), me).start()
+
+        gx_ref[:, columns(c)] = dot(rm(), grad_first, ((0,), (0,))).astype(BF16)
+        mixed = back_in[0, c].reshape(rows, w).astype(F32)
+        gate = gate_ref[:, columns(c)].astype(F32)
+        gout = gout_ref[:, columns(c)].astype(F32)
+        sig = jax.nn.sigmoid(gate)
+        ggate_ref[:, columns(c)] = (gout * mixed * sig * (1.0 + gate * (1.0 - sig))).astype(BF16)
+
+    def left_copy(to, slot):
+        return remote(left_out, left_in.at[slot], left_send.at[to // PEERS], left_recv.at[slot], to)
+
+    def gl_copy(to_slot, to, slot):
+        return remote(
+            gl_out.at[to_slot], gl_in.at[slot], gl_send.at[to_slot], gl_recv.at[slot], to
+        )
+
+    for load in loads:
+        load.wait()
+    compute_a(0)
+    eye = (iota((rows, rows), 0) == iota((rows, rows), 1)).astype(BF16)
+    left_out[...] = dot(left_ref[...], eye, ((0,), (0,))).astype(BF16)
+    pl.semaphore_wait(barrier, n - 1)
+    for plane in range(PLANES):
+        to = PEERS * plane + z
+
+        @pl.when(to != me)
+        def _(to=to):
+            left_copy(to, i).start()
+
+        @pl.when(to == me)
+        def _():
+            left_in[i] = left_out[...]
+
+    send_a(0)
+    if parts > 1:
+        compute_a(1)
+        send_a(1)
+    gram[...] = jnp.zeros_like(gram)
+    term[...] = jnp.zeros_like(term)
+
+    size = n * jj
+
+    def pick():
+        row, col = iota((size, size), 0), iota((size, size), 1)
+        return col == (row % jj) * n + row // jj
+
+    def spread():
+        return iota((n, size), 1) // jj == iota((n, size), 0)
+
+    def keep():
+        row, col = iota((size, size), 0), iota((size, size), 1)
+        return (row % jj == col % jj) & (row // jj >= col // jj)
+
+    for s in range(PEERS):
+        src = PEERS * i + s
+
+        @pl.when(src != me)
+        def _(src=src, s=s):
+            left_copy(src, s).wait_recv()
+
+    left_all = jnp.concatenate([left_in[s] for s in range(PEERS)], axis=1)
+    picked = dot(pick().astype(BF16), left_all, ((1,), (1,))).astype(BF16)
+    weights[...] = jnp.where(keep(), dot(picked, spread().astype(BF16)), 0.0).astype(BF16)
+
+    def left_grads():
+        best = lax.Precision.HIGHEST
+        summed = dot(
+            jnp.where(keep(), gram[...], 0.0), spread().astype(F32), ((1,), (1,)), precision=best
+        )
+        flat = dot(summed, pick().astype(F32), ((0,), (0,)), precision=best)
+        each = size // PEERS
+        for s in range(PEERS):
+            gl_out[s] = flat[:, s * each : (s + 1) * each]
+            to = PEERS * i + s
+
+            @pl.when(to != me)
+            def _(to=to, s=s):
+                gl_copy(s, to, z).start()
+
+            @pl.when(to == me)
+            def _(s=s):
+                gl_in[z] = gl_out[s]
+
+    def at(cond, stage, c):
+        @pl.when(cond)
+        def _():
+            stage(c)
+
+    def a_part(c):
+        compute_a(c)
+        send_a(c)
+
+    @pl.loop(0, parts + 3)
+    def _(t):
+        at(t < parts, stage_b, t)
+        at(t < parts - 2, a_part, t + 2)
+        at((t >= 1) & (t <= parts), stage_d, t - 1)
+        at((t >= 2) & (t <= parts + 1), stage_s, t - 2)
+
+        @pl.when(t == parts)
+        def _():
+            left_grads()
+
+        at(t >= 3, stage_e, t - 3)
+
+    for plane in range(PLANES):
+        src = PEERS * plane + z
+
+        @pl.when(src != me)
+        def _(src=src, plane=plane):
+            gl_copy(0, src, plane).wait_recv()
+
+    total = gl_in[0] + gl_in[1] + gl_in[2] + gl_in[3]
+    gleft_ref[...] = total.T
+
+    @pl.loop(1, n)
+    def _(k):
+        src = lax.rem(me + n - k, n)
+        term_copy(src, src).wait_recv()
+
+    term_in[me] = term_out[me]
+    gright_ref[...] = jnp.sum(term_in[...], axis=0)
+
+    @pl.loop(0, parts)
+    def _(c):
+        for k in range(1, PEERS):
+            p = lax.rem(i + k, PEERS)
+            for kind in range(2):
+                a_copy(kind, c, p).wait_send()
+                b_copy(kind, c, p, i).wait_send()
+        for q, (kind, targets) in relays.items():
+
+            @pl.when(z == q)
+            def _(q=q, kind=kind, targets=targets):
+                for slot, to_plane in enumerate(targets):
+                    relay(kind, c, q, slot, to_plane).wait_send()
+
+        @pl.when((z == 1) | (z == 2))
+        def _():
+            sums(c, 0).wait_send()
+
+    for plane in range(PLANES):
+        to = PEERS * plane + z
+
+        @pl.when(to != me)
+        def _(to=to):
+            left_copy(to, i).wait_send()
+
+    for s in range(PEERS):
+        to = PEERS * i + s
+
+        @pl.when(to != me)
+        def _(to=to, s=s):
+            gl_copy(s, to, z).wait_send()
+
+    @pl.loop(1, n)
+    def _(k):
+        term_copy(lax.rem(me + k, n), me).wait_send()
+
+
+def fused_shards(parts, inputs, gate_in, grad_out, right_factor, left_factor):
+    rows, width = inputs.shape
+    n = PLANES * PEERS
+    r, jj, w = rows // n, rows // PEERS, width // parts
+    left2 = left_factor.reshape(r * n, n)
+    vmem = pl.BlockSpec(memory_space=pltpu.VMEM)
+    hbm = pl.BlockSpec(memory_space=pl.ANY)
+    dma = pltpu.SemaphoreType.DMA
+    gx, gg, gr, gl = pl.pallas_call(
+        functools.partial(kernel, parts),
+        out_shape=(
+            jax.ShapeDtypeStruct(inputs.shape, BF16),
+            jax.ShapeDtypeStruct(inputs.shape, BF16),
+            jax.ShapeDtypeStruct((r, rows), F32),
+            jax.ShapeDtypeStruct((r * n, n), F32),
+        ),
+        in_specs=[hbm] * 5,
+        out_specs=(vmem,) * 4,
+        scratch_shapes=[
+            pltpu.VMEM(inputs.shape, BF16),
+            pltpu.VMEM(inputs.shape, BF16),
+            pltpu.VMEM(inputs.shape, BF16),
+            pltpu.VMEM(right_factor.shape, BF16),
+            pltpu.VMEM(left2.shape, BF16),
+            pltpu.VMEM((2, parts, PEERS, jj, w), BF16),
+            pltpu.VMEM((2, parts, n, jj, w), BF16),
+            pltpu.VMEM((2, parts, PEERS, jj, w), BF16),
+            pltpu.VMEM((2, parts, PEERS, jj, w), BF16),
+            pltpu.VMEM((parts, PEERS, jj, w), SUMS),
+            pltpu.VMEM((parts, PEERS, jj, w), SUMS),
+            pltpu.VMEM((n * jj, n * jj), BF16),
+            pltpu.VMEM((n * jj, n * jj), F32),
+            pltpu.VMEM((rows, rows), F32),
+            pltpu.VMEM((n, r * n), BF16),
+            pltpu.VMEM((PEERS, n, r * n), BF16),
+            pltpu.VMEM((PEERS, n, r * n), F32),
+            pltpu.VMEM((PLANES, n, r * n), F32),
+            pltpu.VMEM((n, r, rows), F32),
+            pltpu.VMEM((n, r, rows), F32),
+            dma((5,)),
+            dma((2, parts, PEERS)),
+            dma((2, parts, PEERS)),
+            dma((parts, 2)),
+            dma((2, parts, PLANES)),
+            dma((parts,)),
+            dma((parts,)),
+            dma((2, parts, PEERS)),
+            dma((2, parts, PEERS)),
+            dma((PLANES,)),
+            dma((PEERS,)),
+            dma((PEERS,)),
+            dma((PLANES,)),
+            dma((n,)),
+            dma((n,)),
+        ],
+        compiler_params=pltpu.CompilerParams(
+            collective_id=0, has_side_effects=True, vmem_limit_bytes=56 * 2**20
+        ),
+    )(inputs, gate_in, grad_out, right_factor, left2)
+    return gx, gg, gr, gl.reshape(r, n, n)
+
+
 def solution(mesh):
+    n = mesh.shape["seqa"]
+
+    def shards(inputs, gate_in, grad_out, right_factor, left_factor):
+        rows = inputs.shape[0]
+        if n == PLANES * PEERS and rows == 128 and left_factor.shape == (8, n, n):
+            return fused_shards(PARTS, inputs, gate_in, grad_out, right_factor, left_factor)
+        return plain_shards(inputs, gate_in, grad_out, right_factor, left_factor)
+
     in_specs = (
         P(("groups", "seqa"), None),
         P(("groups", "seqa"), None),

time: 199 us -> 59.5 us (0.30)
  waiting for transfers between devices: 108 us -> 0 us
  Pallas kernels: 0 us -> 54.8 us
  blocking collectives: 36.9 us -> 0 us
  between operations: 14.8 us -> 0.65 us
  starting transfers between devices: 11.5 us -> 0 us
  other arithmetic: 9.03 us -> 0 us
  local copies, waits for them, and re-layouts: 11.8 us -> 3.97 us
  matrix products: 5.72 us -> 0 us
    unnamed x2 -> x0, waiting for transfers between devices: 82.2 us -> none
    pallas_call x0 -> x1, Pallas kernels: none -> 54.8 us  [fused_shards(): pl.pallas_call(functools.partial(kernel, parts), out_shape=(jax.ShapeDtyp...]
    all_to_all x2 -> x0, blocking collectives: 36.9 us -> none  [the longest x1 18.5 us: shards(): lax.all_to_all(second, 'seqa', split_axis=0, concat_axis=1, tiled=True)[0]]
    all_to_all x2 -> x0, waiting for transfers between devices: 25.7 us -> none  [the longest x1 14.5 us: shards(): lax.all_to_all(first[None], 'seqa', split_axis=1, concat_axis=0, tiled=True)]
    all_to_all x2 -> x0, starting transfers between devices: 11.5 us -> none  [the longest x1 7.39 us: shards(): lax.all_to_all(first[None], 'seqa', split_axis=1, concat_axis=0, tiled=True)]
    unnamed x2 -> x0, other arithmetic: 7.67 us -> none
    dot_general x6 -> x0, matrix products: 5.72 us -> none  [the longest x1 1.29 us: shards(): jnp.einsum('pjd,ajd->jpa', grad_cols, first_cols, preferred_element_type=...]
    unnamed x21 -> x10, local copies, waits for them, and re-layouts: 8.78 us -> 3.97 us
  transfers between devices with their start and end apart: 3 -> 0, of which waited for: 3 -> 0; matrix products, arithmetic and copies ran while one was open for 2% -> 0% of each run, Pallas kernels for 0% -> 0%
where the time goes in v2:
time: 59.5 us; the launch traced here: 59.4 us
  Pallas kernels  54.8 us (92%)
  local copies, waits for them, and re-layouts  3.97 us (7%)
  between operations  0.65 us (1%)
    pallas_call x1, Pallas kernels, fused_shards(): pl.pallas_call(functools.partial(kernel, parts), out_shape=(jax.ShapeDtyp...  54.8 us
    unnamed x10, local copies, waits for them, and re-layouts  3.97 us

profile of v2, /device:TPU:0, one launch (start us, length us, event | category | flops | bytes accessed | tf_op | source)
XLA Modules:
  0.0 59.4 jit_solution(13381530904642878438)
XLA Ops:
  0.6 54.8 %shard_map.84 = (bf16[128,2048]{1,0:T(8,128)(2,1)}, bf16[128,2048]{1,0:T(8,128)(2,1)}, f32[8,128]{1,0:T(8,128)}, f32[128,16]{1,0:T(8,128)}) custom-call(bf16[128,2048]{1,0:T(8,128)(2,1)} %x_hbm.1, bf16[128,2048]{1,0:T(8,128)(2,1)} %gate_hbm.1, bf16[128,2048]{1,0:T(8,128)(2,1)} %gout_hbm.1, bf16[128,128]{1,0:T(8,128)(2,1)} %right_hbm.1, bf16[128,16]{1,0:T(8,128)(2,1)} %bitcast.3), custom_call_target="tpu_custom_call" | custom-call | tf_op jit(solution)/shard_map/pallas_call | solution.py:426
  55.4 0.0 copy-start
  55.4 1.9 %copy.13 = bf16[128,2048]{1,0:T(8,128)(2,1)} copy(bf16[128,2048]{1,0:T(8,128)(2,1)} %get-tuple-element.16) | data formatting | bytes 1048576
  57.3 0.0 copy-done
  57.3 0.0 copy-start.2
  57.3 0.0 copy-start.1
  57.4 0.8 %copy.14 = bf16[128,2048]{1,0:T(8,128)(2,1)} copy(bf16[128,2048]{1,0:T(8,128)(2,1)S(1)} %copy-done) | data formatting | bytes 1048576
  58.1 0.0 copy-done.2
  58.1 0.6 copy.15
  58.7 0.0 copy-done.1
  58.7 0.6 %copy.16 = f32[8,16,16]{2,1,0:T(8,128)} copy(f32[8,16,16]{2,1,0:T(8,128)S(1)} %bitcast.2) | data formatting | bytes 16384
Async XLA Ops:
  55.4 2.0 %copy-start = (bf16[128,2048]{1,0:T(8,128)(2,1)S(1)}, bf16[128,2048]{1,0:T(8,128)(2,1)}, u32[]{:S(2)}) copy-start(bf16[128,2048]{1,0:T(8,128)(2,1)} %get-tuple-element.17) | copy-start | bytes 1572868
  57.3 0.8 %copy-start.2 = (f32[8,128]{1,0:T(8,128)S(1)}, f32[8,128]{1,0:T(8,128)}, u32[]{:S(2)}) copy-start(f32[8,128]{1,0:T(8,128)} %get-tuple-element.18) | copy-start | bytes 12292
  57.3 1.4 %copy-start.1 = (f32[128,16]{1,0:T(8,128)S(1)}, f32[128,16]{1,0:T(8,128)}, u32[]{:S(2)}) copy-start(f32[128,16]{1,0:T(8,128)} %get-tuple-element.11) | copy-start | bytes 24580

commit v3 on v2

--- a/solution.py
+++ b/solution.py
@@ -8,8 +8,8 @@
 from jax.sharding import PartitionSpec as P
 
 F32, BF16 = jnp.float32, jnp.bfloat16
-PARTS = 4
-SUMS = F32
+PARTS = 8
+SUMS = BF16
 
 
 def gate_grads(mixed, gate_in, grad_out):
@@ -56,6 +56,9 @@
     return (grad_inputs, grad_gate, grad_right, grad_left)
 
 
+AHEAD = 2
+
+
 def iota(shape, dim):
     return lax.broadcasted_iota(jnp.int32, shape, dim)
 
@@ -72,7 +75,7 @@
     parts, x_hbm, gate_hbm, gout_hbm, right_hbm, left_hbm,
     gx_ref, ggate_ref, gright_ref, gleft_ref,
     x_ref, gate_ref, gout_ref, right_ref, left_ref,
-    cols_out, cols, back_out, back_in, sums_out, sums_in, weights, gram, term,
+    cols_out, cols, back_out, back_in, sums_out, sums_in, weights, weights_t, rights, gram, term,
     left_out, left_in, gl_out, gl_in, term_out, term_in,
     load_sem, a_send, a_recv, relay_send, relay_recv, sum_send, sum_recv, b_send, b_recv,
     left_send, left_recv, gl_send, gl_recv, t_send, t_recv,
@@ -112,14 +115,15 @@
 
     causal = iota((rows, rows), 0) >= iota((rows, rows), 1)
 
-    def rm():
-        return jnp.where(causal, right_ref[...].astype(F32), 0.0).astype(BF16)
 
     def block(kind, c, q):
         return cols.at[kind, c, pl.ds(PEERS * q, PEERS)]
 
     def planes(kind, c, lo, hi):
         return cols[kind, c, PEERS * lo : PEERS * hi].reshape((hi - lo) * m, w)
+
+    def wt_block(q0, q1, p0, p1):
+        return weights_t[m * q0 : m * q1, m * p0 : m * p1]
 
     def w_block(p0, p1, q0, q1):
         return weights[m * p0 : m * p1, m * q0 : m * q1]
@@ -137,21 +141,21 @@
         )
 
     def compute_a(c):
-        first = dot(rm(), x_ref[:, columns(c)])
+        first = dot(rights[0], x_ref[:, columns(c)])
         cols_out[0, c] = first.astype(BF16).reshape(PEERS, jj, w)
         gate = gate_ref[:, columns(c)].astype(F32)
         gout = gout_ref[:, columns(c)].astype(F32)
         mixed_grad = gout * gate * jax.nn.sigmoid(gate)
         cols_out[1, c] = mixed_grad.astype(BF16).reshape(PEERS, jj, w)
+        for kind in range(2):
+            cols[kind, c, me] = cols_out[kind, c, i]
 
     def send_a(c):
         for k in range(1, PEERS):
             for kind in range(2):
                 a_copy(kind, c, lax.rem(i + k, PEERS)).start()
-        for kind in range(2):
-            cols[kind, c, me] = cols_out[kind, c, i]
-
-    relays = {0: (0, (1, 2)), 1: (0, (2,)), 2: (1, (1,)), 3: (1, (2, 1))}
+
+    relays = {0: (0, (2, 1)), 1: (0, (2,)), 2: (1, (1,)), 3: (1, (1, 2))}
 
     def relay(kind, c, q, slot, to_plane):
         return remote(
@@ -181,7 +185,7 @@
             planes(1, c, p0, p1), planes(0, c, q0, q1), ((1,), (1,))
         )
 
-    def stage_b(c):
+    def start_relays(c):
         for k in range(1, PEERS):
             for kind in range(2):
                 a_arrival(kind, c, lax.rem(i + PEERS - k, PEERS)).wait_recv()
@@ -191,12 +195,17 @@
             def _(q=q, kind=kind, targets=targets):
                 for slot, to_plane in enumerate(targets):
                     relay(kind, c, q, slot, to_plane).start()
-                if q == 0:
-                    send_back(0, c, dot(w_block(0, 1, 0, 1), planes(0, c, 0, 1)))
-                    add_gram(c, 0, 1, 0, 1)
-                if q == 3:
-                    send_back(1, c, dot(w_block(3, 4, 3, 4), planes(1, c, 3, 4), ((0,), (0,))))
-                    add_gram(c, 3, 4, 3, 4)
+
+    def stage_b(c):
+        @pl.when(z == 0)
+        def _():
+            send_back(0, c, dot(w_block(0, 1, 0, 1), planes(0, c, 0, 1)))
+            add_gram(c, 0, 1, 0, 1)
+
+        @pl.when(z == 3)
+        def _():
+            send_back(1, c, dot(wt_block(3, 4, 3, 4), planes(1, c, 3, 4)))
+            add_gram(c, 3, 4, 3, 4)
 
     def stage_d(c):
         @pl.when(z == 1)
@@ -206,20 +215,21 @@
             relay(1, c, 2, 0, 2).wait_recv()
             relay(1, c, 3, 0, 3).wait_recv()
             g = planes(1, c, 1, 4)
-            sums_out[c] = dot(w_block(1, 4, 0, 1), g, ((0,), (0,))).reshape(PEERS, jj, w)
+            summed = dot(wt_block(0, 1, 1, 4), g)
+            sums_out[c] = summed.astype(SUMS).reshape(PEERS, jj, w)
             sums(c, 0).start()
-            send_back(1, c, dot(w_block(1, 4, 1, 2), g, ((0,), (0,))))
+            send_back(1, c, dot(wt_block(1, 2, 1, 4), g))
             add_gram(c, 1, 4, 0, 1)
             add_gram(c, 1, 2, 1, 2)
 
         @pl.when(z == 2)
         def _():
             relay(1, c, 3, 0, 3).wait_recv()
-            send_back(1, c, dot(w_block(2, 4, 2, 3), planes(1, c, 2, 4), ((0,), (0,))))
+            send_back(1, c, dot(wt_block(2, 3, 2, 4), planes(1, c, 2, 4)))
             relay(0, c, 1, 0, 1).wait_recv()
             relay(0, c, 0, 0, 0).wait_recv()
             f = planes(0, c, 0, 3)
-            sums_out[c] = dot(w_block(3, 4, 0, 3), f).reshape(PEERS, jj, w)
+            sums_out[c] = dot(w_block(3, 4, 0, 3), f).astype(SUMS).reshape(PEERS, jj, w)
             sums(c, 3).start()
             send_back(0, c, dot(w_block(2, 3, 0, 3), f))
             add_gram(c, 2, 4, 1, 3)
@@ -227,7 +237,7 @@
     def stage_s(c):
         @pl.when(z == 0)
         def _():
-            own = dot(w_block(0, 1, 0, 1), planes(1, c, 0, 1), ((0,), (0,)))
+            own = dot(wt_block(0, 1, 0, 1), planes(1, c, 0, 1))
             sums(c, 1).wait_recv()
             send_back(1, c, own + sums_in[c].reshape(m, w))
 
@@ -256,7 +266,7 @@
             def _(k):
                 term_copy(lax.rem(me + k, n), me).start()
 
-        gx_ref[:, columns(c)] = dot(rm(), grad_first, ((0,), (0,))).astype(BF16)
+        gx_ref[:, columns(c)] = dot(rights[1], grad_first).astype(BF16)
         mixed = back_in[0, c].reshape(rows, w).astype(F32)
         gate = gate_ref[:, columns(c)].astype(F32)
         gout = gout_ref[:, columns(c)].astype(F32)
@@ -273,10 +283,17 @@
 
     for load in loads:
         load.wait()
-    compute_a(0)
+    right = jnp.where(causal, right_ref[...].astype(F32), 0.0)
+    rights[0] = right.astype(BF16)
+    rights[1] = right.T.astype(BF16)
+    for c in range(parts):
+        compute_a(c)
+    gram[...] = jnp.zeros_like(gram)
+    term[...] = jnp.zeros_like(term)
     eye = (iota((rows, rows), 0) == iota((rows, rows), 1)).astype(BF16)
     left_out[...] = dot(left_ref[...], eye, ((0,), (0,))).astype(BF16)
     pl.semaphore_wait(barrier, n - 1)
+    send_a(0)
     for plane in range(PLANES):
         to = PEERS * plane + z
 
@@ -288,12 +305,9 @@
         def _():
             left_in[i] = left_out[...]
 
-    send_a(0)
-    if parts > 1:
-        compute_a(1)
-        send_a(1)
-    gram[...] = jnp.zeros_like(gram)
-    term[...] = jnp.zeros_like(term)
+    for c in range(1, min(AHEAD, parts)):
+        send_a(c)
+    start_relays(0)
 
     size = n * jj
 
@@ -318,6 +332,7 @@
     left_all = jnp.concatenate([left_in[s] for s in range(PEERS)], axis=1)
     picked = dot(pick().astype(BF16), left_all, ((1,), (1,))).astype(BF16)
     weights[...] = jnp.where(keep(), dot(picked, spread().astype(BF16)), 0.0).astype(BF16)
+    weights_t[...] = weights[...].T
 
     def left_grads():
         best = lax.Precision.HIGHEST
@@ -343,14 +358,11 @@
         def _():
             stage(c)
 
-    def a_part(c):
-        compute_a(c)
-        send_a(c)
-
     @pl.loop(0, parts + 3)
     def _(t):
+        at(t < parts - AHEAD, send_a, t + AHEAD)
+        at(t < parts - 1, start_relays, t + 1)
         at(t < parts, stage_b, t)
-        at(t < parts - 2, a_part, t + 2)
         at((t >= 1) & (t <= parts), stage_d, t - 1)
         at((t >= 2) & (t <= parts + 1), stage_s, t - 2)
 
@@ -446,6 +458,8 @@
             pltpu.VMEM((parts, PEERS, jj, w), SUMS),
             pltpu.VMEM((parts, PEERS, jj, w), SUMS),
             pltpu.VMEM((n * jj, n * jj), BF16),
+            pltpu.VMEM((n * jj, n * jj), BF16),
+            pltpu.VMEM((2, rows, rows), BF16),
             pltpu.VMEM((n * jj, n * jj), F32),
             pltpu.VMEM((rows, rows), F32),
             pltpu.VMEM((n, r * n), BF16),

time: 59.5 us -> 55.3 us (0.929)
  Pallas kernels: 54.8 us -> 50.5 us
    pallas_call x1, Pallas kernels: 54.8 us -> 50.5 us  [fused_shards(): pl.pallas_call(functools.partial(kernel, parts), out_shape=(jax.ShapeDtyp...]
where the time goes in v3:
time: 55.3 us; the launch traced here: 55.2 us
  Pallas kernels  50.5 us (91%)
  local copies, waits for them, and re-layouts  3.97 us (7%)
  between operations  0.65 us (1%)
    pallas_call x1, Pallas kernels, fused_shards(): pl.pallas_call(functools.partial(kernel, parts), out_shape=(jax.ShapeDtyp...  50.5 us
    unnamed x10, local copies, waits for them, and re-layouts  3.97 us

profile of v3, /device:TPU:0, one launch (start us, length us, event | category | flops | bytes accessed | tf_op | source)
XLA Modules:
  0.0 55.2 jit_solution(15481374258098456037)
XLA Ops:
  0.6 50.5 %shard_map.84 = (bf16[128,2048]{1,0:T(8,128)(2,1)}, bf16[128,2048]{1,0:T(8,128)(2,1)}, f32[8,128]{1,0:T(8,128)}, f32[128,16]{1,0:T(8,128)}) custom-call(bf16[128,2048]{1,0:T(8,128)(2,1)} %x_hbm.1, bf16[128,2048]{1,0:T(8,128)(2,1)} %gate_hbm.1, bf16[128,2048]{1,0:T(8,128)(2,1)} %gout_hbm.1, bf16[128,128]{1,0:T(8,128)(2,1)} %right_hbm.1, bf16[128,16]{1,0:T(8,128)(2,1)} %bitcast.3), custom_call_target="tpu_custom_call" | custom-call | tf_op jit(solution)/shard_map/pallas_call | solution.py:438
  51.2 0.0 copy-start
  51.2 1.9 %copy.13 = bf16[128,2048]{1,0:T(8,128)(2,1)} copy(bf16[128,2048]{1,0:T(8,128)(2,1)} %get-tuple-element.16) | data formatting | bytes 1048576
  53.1 0.0 copy-done
  53.1 0.0 copy-start.2
  53.1 0.0 copy-start.1
  53.1 0.8 %copy.14 = bf16[128,2048]{1,0:T(8,128)(2,1)} copy(bf16[128,2048]{1,0:T(8,128)(2,1)S(1)} %copy-done) | data formatting | bytes 1048576
  53.9 0.0 copy-done.2
  53.9 0.6 %copy.15 = f32[8,128]{1,0:T(8,128)} copy(f32[8,128]{1,0:T(8,128)S(1)} %copy-done.2) | data formatting | bytes 8192
  54.5 0.0 copy-done.1
  54.5 0.6 %copy.16 = f32[8,16,16]{2,1,0:T(8,128)} copy(f32[8,16,16]{2,1,0:T(8,128)S(1)} %bitcast.2) | data formatting | bytes 16384
Async XLA Ops:
  51.2 2.0 %copy-start = (bf16[128,2048]{1,0:T(8,128)(2,1)S(1)}, bf16[128,2048]{1,0:T(8,128)(2,1)}, u32[]{:S(2)}) copy-start(bf16[128,2048]{1,0:T(8,128)(2,1)} %get-tuple-element.17) | copy-start | bytes 1572868
  53.1 0.8 %copy-start.2 = (f32[8,128]{1,0:T(8,128)S(1)}, f32[8,128]{1,0:T(8,128)}, u32[]{:S(2)}) copy-start(f32[8,128]{1,0:T(8,128)} %get-tuple-element.18) | copy-start | bytes 12292
  53.1 1.4 %copy-start.1 = (f32[128,16]{1,0:T(8,128)S(1)}, f32[128,16]{1,0:T(8,128)}, u32[]{:S(2)}) copy-start(f32[128,16]{1,0:T(8,128)} %get-tuple-element.11) | copy-start | bytes 24580

commit v4 on v3

--- a/solution.py
+++ b/solution.py
@@ -366,7 +366,7 @@
         at((t >= 1) & (t <= parts), stage_d, t - 1)
         at((t >= 2) & (t <= parts + 1), stage_s, t - 2)
 
-        @pl.when(t == parts)
+        @pl.when(t == parts + 1)
         def _():
             left_grads()
 

time: 55.3 us -> 55.3 us (level)
  no operation moved by 1% of the time
where the time goes in v4:
time: 55.3 us; the launch traced here: 55.2 us
  Pallas kernels  50.5 us (91%)
  local copies, waits for them, and re-layouts  3.97 us (7%)
  between operations  0.65 us (1%)
    pallas_call x1, Pallas kernels, fused_shards(): pl.pallas_call(functools.partial(kernel, parts), out_shape=(jax.ShapeDtyp...  50.5 us
    unnamed x10, local copies, waits for them, and re-layouts  3.97 us

profile of v4, /device:TPU:0, one launch (start us, length us, event | category | flops | bytes accessed | tf_op | source)
XLA Modules:
  0.0 55.2 jit_solution(6842277366723492129)
XLA Ops:
  0.6 50.5 %shard_map.84 = (bf16[128,2048]{1,0:T(8,128)(2,1)}, bf16[128,2048]{1,0:T(8,128)(2,1)}, f32[8,128]{1,0:T(8,128)}, f32[128,16]{1,0:T(8,128)}) custom-call(bf16[128,2048]{1,0:T(8,128)(2,1)} %x_hbm.1, bf16[128,2048]{1,0:T(8,128)(2,1)} %gate_hbm.1, bf16[128,2048]{1,0:T(8,128)(2,1)} %gout_hbm.1, bf16[128,128]{1,0:T(8,128)(2,1)} %right_hbm.1, bf16[128,16]{1,0:T(8,128)(2,1)} %bitcast.3), custom_call_target="tpu_custom_call" | custom-call | tf_op jit(solution)/shard_map/pallas_call | solution.py:438
  51.2 0.0 copy-start
  51.2 1.9 %copy.13 = bf16[128,2048]{1,0:T(8,128)(2,1)} copy(bf16[128,2048]{1,0:T(8,128)(2,1)} %get-tuple-element.16) | data formatting | bytes 1048576
  53.1 0.0 copy-done
  53.1 0.0 copy-start.2
  53.1 0.0 copy-start.1
  53.1 0.8 %copy.14 = bf16[128,2048]{1,0:T(8,128)(2,1)} copy(bf16[128,2048]{1,0:T(8,128)(2,1)S(1)} %copy-done) | data formatting | bytes 1048576
  53.9 0.0 copy-done.2
  53.9 0.6 %copy.15 = f32[8,128]{1,0:T(8,128)} copy(f32[8,128]{1,0:T(8,128)S(1)} %copy-done.2) | data formatting | bytes 8192
  54.5 0.0 copy-done.1
  54.5 0.6 %copy.16 = f32[8,16,16]{2,1,0:T(8,128)} copy(f32[8,16,16]{2,1,0:T(8,128)S(1)} %bitcast.2) | data formatting | bytes 16384
Async XLA Ops:
  51.2 2.0 %copy-start = (bf16[128,2048]{1,0:T(8,128)(2,1)S(1)}, bf16[128,2048]{1,0:T(8,128)(2,1)}, u32[]{:S(2)}) copy-start(bf16[128,2048]{1,0:T(8,128)(2,1)} %get-tuple-element.17) | copy-start | bytes 1572868
  53.1 0.8 %copy-start.2 = (f32[8,128]{1,0:T(8,128)S(1)}, f32[8,128]{1,0:T(8,128)}, u32[]{:S(2)}) copy-start(f32[8,128]{1,0:T(8,128)} %get-tuple-element.18) | copy-start | bytes 12292
  53.1 1.4 %copy-start.1 = (f32[128,16]{1,0:T(8,128)S(1)}, f32[128,16]{1,0:T(8,128)}, u32[]{:S(2)}) copy-start(f32[128,16]{1,0:T(8,128)} %get-tuple-element.11) | copy-start | bytes 24580
